TPU v7x, 512 devices: a whole 4x8x8 slice. The times are simulated.
512 devices in a mesh: blk: 128 (over z_hi, x, y), grp: 4 (over z_lo, core).
Axes of the slice: x: 4, y: 8, z: 8 (z_hi: 4, z_lo: 2; z = z_hi * 2 + z_lo), core: 2. Of those that a mesh axis runs over, the one named last changes fastest.
Arguments:
- embeddings: bfloat16 [131072, 1024], P(('blk', 'grp')), may hold values from -1 to 1
Outputs:
- density: float32 [131072], P(('blk', 'grp'))
All inputs are finite; a program needn't handle non-finite values.
Results may differ from a plain program's by a relative error of at most 0.0003.
Values may be sent and summed in bfloat16 or wider, within the bound.
A program may use at most 64 MiB of HBM per device.

v0:
```python
import jax
import jax.numpy as jnp
from jax import lax
from jax.sharding import PartitionSpec as P

STOPS = 4


sharpness = 4.0


def from_behind(block, axis, distance):
    devices = range(lax.axis_size(axis))
    route = [((i - distance) % len(devices), i) for i in devices]
    return lax.ppermute(block, axis, route)


def squared_norms(vectors):
    return jnp.einsum("rd,rd->r", vectors, vectors, preferred_element_type=jnp.float32)


def kernel_tile(queries, query_norms, targets):
    target_norms = squared_norms(targets)
    products = lax.dot_general(
        queries, targets, (((1,), (1,)), ((), ())), preferred_element_type=jnp.float32
    )
    distance = query_norms[:, None] + target_norms[None, :] - 2.0 * products
    return jnp.exp(-sharpness * distance)


def body(embeddings):
    block_rows = embeddings.shape[0]
    own_norms = squared_norms(embeddings)
    group_block = lax.all_gather(embeddings, "grp", axis=0, tiled=True)
    first = kernel_tile(embeddings, own_norms, group_block)
    col_index = lax.broadcasted_iota(jnp.int32, first.shape, 1)
    row_index = lax.broadcasted_iota(jnp.int32, first.shape, 0) + lax.axis_index("grp") * block_rows
    first = jnp.where(col_index == row_index, jnp.float32(0.0), first)
    totals = jnp.sum(first, axis=1)
    travel = group_block
    for stop_index in range(1, STOPS):
        travel = from_behind(travel, "blk", 1)
        kernel = kernel_tile(embeddings, own_norms, travel)
        totals = totals + jnp.sum(kernel, axis=1)
        columns = jnp.sum(kernel, axis=0)
        share_sum = lax.psum_scatter(columns, "grp", scatter_dimension=0, tiled=True)
        totals = totals + from_behind(share_sum, "blk", -stop_index)
    return jnp.log1p(totals)


def solution(mesh):
    in_specs = (P(("blk", "grp"), None),)
    out_specs = P(("blk", "grp"))
    return jax.shard_map(body, mesh=mesh, in_specs=in_specs, out_specs=out_specs, check_vma=False)
```

profile of v0, /device:TPU:1, one launch (start us, length us, event | category | flops | bytes accessed | tf_op | source)
XLA Modules:
  0.0 378.2 jit_solution(675964329456198196)
XLA Ops:
  6.5 0.0 all-gather.2.cloned.1.call-start
  6.5 0.7 all-gather.2.cloned.1.call-update
  7.3 42.8 %all-gather.2.cloned.1.call-done = bf16[1024,1024]{1,0:T(8,128)(2,1)} async-done(((bf16[256,1024]{1,0:T(8,128)(2,1)}), bf16[1024,1024]{1,0:T(8,128)(2,1)}) %all-gather.2.cloned.1.call-update) | async-done | bytes 2097168 | tf_op jit(solution)/shard_map/all_gather | solution.py:34
  50.0 3.1 collective-permute-start
  53.1 97.2 %collective-permute-done = bf16[1024,1024]{1,0:T(8,128)(2,1)S(1)} collective-permute-done((bf16[1024,1024]{1,0:T(8,128)(2,1)}, bf16[1024,1024]{1,0:T(8,128)(2,1)S(1)}, u32[]{:S(2)}, u32[]{:S(2)}) %collective-permute-start) | collective-permute-done | bytes 2097184 | tf_op jit(solution)/shard_map/ppermute | solution.py:15
  150.3 1.9 collective-permute-start.2
  152.2 96.3 %collective-permute-done.2 = bf16[1024,1024]{1,0:T(8,128)(2,1)} collective-permute-done((bf16[1024,1024]{1,0:T(8,128)(2,1)S(1)}, bf16[1024,1024]{1,0:T(8,128)(2,1)}, u32[]{:S(2)}, u32[]{:S(2)}) %collective-permute-start.2) | collective-permute-done | bytes 2097184 | tf_op jit(solution)/shard_map/ppermute | solution.py:15
  248.5 1.9 collective-permute-start.4
  250.4 1.3 dynamic-slice
  252.4 1.2 fusion.9
  253.6 0.0 copy-start
  253.6 2.1 fusion.3
  255.7 0.5 fusion.2
  256.2 0.0 copy-done
  256.2 0.7 convolution_multiply_fusion.2
  257.0 2.1 fusion.1
  259.0 2.3 convolution_multiply_fusion.1
  261.4 82.6 %collective-permute-done.4 = bf16[1024,1024]{1,0:T(8,128)(2,1)} collective-permute-done((bf16[1024,1024]{1,0:T(8,128)(2,1)}, bf16[1024,1024]{1,0:T(8,128)(2,1)}, u32[]{:S(2)}, u32[]{:S(2)}) %collective-permute-start.4) | collective-permute-done | bytes 2097184 | tf_op jit(solution)/shard_map/ppermute | solution.py:15
  344.0 2.1 fusion
  346.1 0.0 copy-start.1
  346.1 3.1 fusion.11
  349.2 11.1 %all-reduce.3 = (f32[1024]{0:T(1024)S(1)}, f32[1024]{0:T(1024)S(1)}, f32[1024]{0:T(1024)S(1)}) all-reduce(f32[1024]{0:T(1024)S(1)} %get-tuple-element.13, f32[1024]{0:T(1024)S(1)} %get-tuple-element.11, f32[1024]{0:T(1024)S(1)} %get-tuple-element.6), channel_id=4, replica_groups=mesh['blk'=128,'grp'=4] {'grp'}, use_global_device_ids=true, to_apply=%region_9.10.clone | all-reduce | flops 3072 | bytes 24576
  360.4 0.1 dynamic-slice.5
  360.4 0.1 dynamic-slice.3
  360.5 0.1 dynamic-slice.1
  360.6 1.9 collective-permute-start.1
  362.5 1.9 collective-permute-start.3
  364.4 1.9 collective-permute-start.5
  366.4 0.0 copy-done.1
  366.4 1.0 fusion.8
  367.4 0.0 collective-permute-done.1
  367.4 0.3 collective-permute-done.3
  367.7 3.1 collective-permute-done.5
  370.8 0.6 add_log-plus-one_fusion
  (1 shorter events, 0.0 us)
Async XLA Ops:
  6.5 43.5 %all-gather.2.cloned.1.call-start = ((), (), s32[]{:S(2)}) async-start(), calls=%async_computation | async-start | bytes 2621440 | tf_op jit(solution)/shard_map/all_gather | solution.py:34
  50.0 100.3 %collective-permute-start = (bf16[1024,1024]{1,0:T(8,128)(2,1)}, bf16[1024,1024]{1,0:T(8,128)(2,1)S(1)}, u32[]{:S(2)}, u32[]{:S(2)}) collective-permute-start(bf16[1024,1024]{1,0:T(8,128)(2,1)} %all-gather.2.cloned.1.call-done), channel_id=1, source_target_pairs={{508,0},{0,4},{4,8},{8,12},{12,16},{16,20},{20,24},{24,28},{28,32}... | collective-permute-start | bytes 6291464 | tf_op jit(solution)/shard_map/ppermute | solution.py:15
  150.3 98.2 %collective-permute-start.2 = (bf16[1024,1024]{1,0:T(8,128)(2,1)S(1)}, bf16[1024,1024]{1,0:T(8,128)(2,1)}, u32[]{:S(2)}, u32[]{:S(2)}) collective-permute-start(bf16[1024,1024]{1,0:T(8,128)(2,1)S(1)} %collective-permute-done), channel_id=1, source_target_pairs={{508,0},{0,4},{4,8},{8,12},{12,16},{16,20},{20,24},{24,28},{28,32}... | collective-permute-start | bytes 6291464 | tf_op jit(solution)/shard_map/ppermute | solution.py:15
  248.5 95.5 %collective-permute-start.4 = (bf16[1024,1024]{1,0:T(8,128)(2,1)}, bf16[1024,1024]{1,0:T(8,128)(2,1)}, u32[]{:S(2)}, u32[]{:S(2)}) collective-permute-start(bf16[1024,1024]{1,0:T(8,128)(2,1)} %collective-permute-done.2), channel_id=1, source_target_pairs={{508,0},{0,4},{4,8},{8,12},{12,16},{16,20},{20,24},{24,28},{28,32}... | collective-permute-start | bytes 6291464 | tf_op jit(solution)/shard_map/ppermute | solution.py:15
  253.6 2.6 copy-start
  346.1 20.3 %copy-start.1 = (bf16[1024,1024]{1,0:T(8,128)(2,1)S(1)}, bf16[1024,1024]{1,0:T(8,128)(2,1)}, u32[]{:S(2)}) copy-start(bf16[1024,1024]{1,0:T(8,128)(2,1)} %all-gather.2.cloned.1.call-done) | copy-start | bytes 6291460
  360.6 6.8 %collective-permute-start.1 = (f32[256]{0:T(256)S(1)}, f32[256]{0:T(256)S(1)}, u32[]{:S(2)}, u32[]{:S(2)}) collective-permute-start(f32[256]{0:T(256)S(1)} %dynamic-slice.1), channel_id=1, source_target_pairs={{4,0},{8,4},{12,8},{16,12},{20,16},{24,20},{28,24},{32,28},{36,32}... | collective-permute-start | bytes 3080 | tf_op jit(solution)/shard_map/ppermute | solution.py:15
  362.5 5.2 %collective-permute-start.3 = (f32[256]{0:T(256)S(1)}, f32[256]{0:T(256)S(1)}, u32[]{:S(2)}, u32[]{:S(2)}) collective-permute-start(f32[256]{0:T(256)S(1)} %dynamic-slice.3), channel_id=1, source_target_pairs={{8,0},{12,4},{16,8},{20,12},{24,16},{28,20},{32,24},{36,28},{40,32... | collective-permute-start | bytes 3080 | tf_op jit(solution)/shard_map/ppermute | solution.py:15
  364.4 6.4 %collective-permute-start.5 = (f32[256]{0:T(256)S(1)}, f32[256]{0:T(256)S(1)}, u32[]{:S(2)}, u32[]{:S(2)}) collective-permute-start(f32[256]{0:T(256)S(1)} %dynamic-slice.5), channel_id=1, source_target_pairs={{12,0},{16,4},{20,8},{24,12},{28,16},{32,20},{36,24},{40,28},{44,3... | collective-permute-start | bytes 3080 | tf_op jit(solution)/shard_map/ppermute | solution.py:15
Sparse Core Ops, SparseCore 0:
  9.5 40.5 all-gather.1
where the time goes:
time: 382 us; the launch traced here: 378 us
  waiting for transfers between devices  323 us (85%)
  between operations  14.2 us (4%)
  starting transfers between devices  12.7 us (3%)
  blocking collectives  11.1 us (3%)
  other arithmetic  8.55 us (2%)
  matrix products  7.24 us (2%)
    ppermute x6, waiting for transfers between devices, from_behind(): return lax.ppermute(block, axis, route)  279 us
    all_gather x1, waiting for transfers between devices, body(): group_block = lax.all_gather(embeddings, 'grp', axis=0, tiled=True)  42.8 us
    ppermute x6, starting transfers between devices, from_behind(): return lax.ppermute(block, axis, route)  12.7 us
    unnamed x1, blocking collectives  11.1 us
    dot_general x5, other arithmetic, squared_norms(): jnp.einsum('rd,rd->r', vectors, vectors, preferred_element_type=jnp.float32)  7.96 us
  transfers between devices with their start and end apart: 7, of which 6 were waited for; matrix products, arithmetic and copies ran while one was open for 3% of the time, Pallas kernels for 0%

commit v1 on v0

v1 whole, which is shorter than its diff:
```python
import functools
import math

import jax
import jax.numpy as jnp
from jax import lax
from jax.experimental import pallas as pl
from jax.experimental.pallas import tpu as pltpu
from jax.sharding import PartitionSpec as P

MESH = pl.DeviceIdType.MESH
SHARPNESS = 4.0
LOG2E = math.log2(math.e)
SCALE = SHARPNESS * LOG2E
CHUNKS = 4
PERIOD = 32

OWN, CROSS, PREV, XPREV = 0, 2, 4, 6


def kernel(n_blk, block, width, x, out, rows, nxt, nxt2, relay, rsum, rnorm, ncol, ncol2, gains, lsem, ssem, rsem):
    p = lax.axis_index("blk")
    g = lax.axis_index("grp")
    h = g // 2
    c = lax.rem(g, 2)
    m = lax.rem(p, PERIOD)
    is_a, is_b = h == 0, h == 1
    first, low, last, high = m == 0, m < 2, m == PERIOD - 1, m >= PERIOD - 2
    has_prev = jnp.logical_not(jnp.logical_and(first, is_b))
    has_nxt = jnp.logical_not(jnp.logical_and(high, is_a))
    has_nxt2 = jnp.logical_or(jnp.logical_and(first, is_a), jnp.logical_and(high, is_b))
    not_last, not_low = jnp.logical_not(last), jnp.logical_not(low)
    low_a, low_b = jnp.logical_and(low, is_a), jnp.logical_and(low, is_b)
    high_a, high_b = jnp.logical_and(high, is_a), jnp.logical_and(high, is_b)
    last_b = jnp.logical_and(last, is_b)
    send_xprev = jnp.logical_or(not_last, is_b)
    send_nxt2 = jnp.logical_or(jnp.logical_and(m == 2, is_b), low_a)
    first_a = jnp.logical_and(first, is_a)
    first_b = jnp.logical_and(first, is_b)

    def dev(dp, hh, cc):
        return (lax.rem(p + dp + n_blk, n_blk), hh * 2 + cc)

    step = block // CHUNKS

    def part(ref, i):
        return ref.at[pl.ds(i * step, step)]

    sems = [0]

    def flow(count):
        base = sems[0]
        sems[0] += count
        return base

    def copy(src, dst, k, device, ks=None):
        return pltpu.make_async_remote_copy(
            src_ref=src, dst_ref=dst, send_sem=ssem.at[k if ks is None else ks], recv_sem=rsem.at[k],
            device_id=device, device_id_type=MESH)

    f_own = flow(1)
    f_cross, f_crossf, f_prev, f_prevf = flow(CHUNKS), flow(CHUNKS), flow(CHUNKS), flow(CHUNKS)
    f_xprev, f_xprevf, f_nxt, f_nxt2, f_relay = flow(CHUNKS), flow(CHUNKS), flow(CHUNKS), flow(CHUNKS), flow(CHUNKS)
    f_gain = flow(10)

    core = dev(0, h, 1 - c)
    parts = range(CHUNKS)
    own_copy = copy(x, rows.at[OWN + c], f_own, core)
    cross = [copy(part(x, i), part(rows.at[CROSS + c], i), f_cross + i, dev(0, 1 - h, c)) for i in parts]
    crossf = [copy(part(rows.at[CROSS + c], i), part(rows.at[CROSS + c], i), f_crossf + i, core) for i in parts]
    prev = [copy(part(x, i), part(rows.at[PREV + c], i), f_prev + i, dev(1, h, c)) for i in parts]
    prev_relay = [copy(part(rows.at[CROSS + c], i), part(rows.at[PREV + c], i), f_prev + i, dev(1, 0, c)) for i in parts]
    prevf = [copy(part(rows.at[PREV + c], i), part(rows.at[PREV + c], i), f_prevf + i, core) for i in parts]
    xprev = [copy(part(x, i), part(rows.at[XPREV + c], i), f_xprev + i, dev(1, 1 - h, c)) for i in parts]
    xprevf = [copy(part(rows.at[XPREV + c], i), part(rows.at[XPREV + c], i), f_xprevf + i, core) for i in parts]
    nxtc = [copy(part(x, i), part(nxt, i), f_nxt + i, dev(-2, h, c)) for i in parts]
    nxt_relay = [copy(part(relay, i), part(nxt, i), f_nxt + i, dev(PERIOD - 2, 1, c)) for i in parts]
    to_relay = [copy(part(rows.at[CROSS + c], i), part(relay, i), f_relay + i, dev(-PERIOD, 1, c)) for i in parts]
    nxt2c = [copy(part(x, i), part(nxt2, i), f_nxt2 + i, dev(-2, 1 - h, c)) for i in parts]

    local = pltpu.make_async_copy(x, rows.at[OWN + c], lsem)
    local.start()

    barrier = pltpu.get_barrier_semaphore()

    def hello(device):
        pl.semaphore_signal(barrier, inc=1, device_id=device, device_id_type=MESH)

    hello(core)
    hello(dev(0, 1 - h, c))
    pl.when(jnp.logical_not(first))(lambda: hello(dev(-1, h, c)))
    pl.when(has_prev)(lambda: hello(dev(-1, 1 - h, c)))
    pl.when(jnp.logical_not(high))(lambda: hello(dev(2, h, c)))
    pl.when(high_b)(lambda: hello(dev(-(PERIOD - 2), 1, c)))
    pl.when(low_b)(lambda: hello(dev(PERIOD, 0, c)))
    pl.when(has_nxt2)(lambda: hello(dev(2, 1 - h, c)))

    def one(flag):
        return jnp.where(flag, 1, 0)

    targets = 2 + one(not_last) + one(send_xprev) + 1 + one(send_nxt2)
    pl.semaphore_wait(barrier, targets)

    for i in parts:
        cross[i].start()
        pl.when(not_last)(prev[i].start)
        pl.when(not_low)(nxtc[i].start)
        pl.when(send_nxt2)(nxt2c[i].start)
        if i == 0:
            own_copy.start()
    for i in parts:
        pl.when(send_xprev)(xprev[i].start)

    rsum[...] = jnp.zeros_like(rsum)

    def squares(block_rows):
        v = block_rows.astype(jnp.float32)
        v = v * v
        total = v[:, 0:128]
        for k in range(1, width // 128):
            total = total + v[:, k * 128:(k + 1) * 128]
        return total

    def flat(acc, weight):
        ones = jnp.full((8, 128), weight, jnp.float32)
        return lax.dot_general(ones, acc, (((1,), (1,)), ((), ())), precision=lax.Precision.HIGHEST,
                               preferred_element_type=jnp.float32)

    def norms(s):
        rnorm[s] = flat(squares(rows[s]), 1.0) * SCALE

    def column_norms(block_rows):
        return jnp.sum(squares(block_rows), axis=1, keepdims=True) * SCALE

    def affinity(targets_, target_norms, s):
        products = lax.dot_general(targets_, rows[s], (((1,), (1,)), ((), ())), preferred_element_type=jnp.float32)
        return jnp.exp2(products * (2.0 * SCALE) - (target_norms + rnorm[s, 0:1, :]))

    def fold(e):
        total = e[:, 0:128]
        for k in range(1, block // 128):
            total = total + e[:, k * 128:(k + 1) * 128]
        return total

    def sweep(ref, lo, hi):
        target = ref[...]
        target_norms = column_norms(target)

        def visit(s, acc):
            e = affinity(target, target_norms, s)
            rsum[s] += jnp.sum(e.reshape(block // 8, 8, block), axis=0)
            return acc + fold(e)

        acc = lax.fori_loop(lo, hi, visit, jnp.zeros((block, 128), jnp.float32))
        return flat(acc, 0.125)

    local.wait()
    norms(OWN + c)

    for i in parts:
        cross[i].wait_recv()
        crossf[i].start()
        pl.when(low_a)(to_relay[i].start)
        pl.when(last_b)(prev_relay[i].start)

    @pl.when(low_b)
    def _():
        for i in parts:
            to_relay[i].wait_recv()
            nxt_relay[i].start()

    @pl.when(has_prev)
    def _():
        for i in parts:
            prev[i].wait_recv()
            prevf[i].start()

    own_copy.wait_recv()
    norms(OWN + 1 - c)
    for i in parts:
        crossf[i].wait_recv()
    norms(CROSS)
    norms(CROSS + 1)

    mine = rows[OWN + c]
    mine_norms = column_norms(mine)
    diagonal = lax.broadcasted_iota(jnp.int32, (block, block), 0) == lax.broadcasted_iota(jnp.int32, (block, block), 1)

    def visit_own(s, acc):
        e = affinity(mine, mine_norms, s)
        e = jnp.where(jnp.logical_and(diagonal, s == OWN + c), 0.0, e)
        return acc + fold(e)

    acc = lax.fori_loop(0, 4, visit_own, jnp.zeros((block, 128), jnp.float32))
    rsum[OWN + c] += flat(acc, 0.125)

    @pl.when(has_prev)
    def _():
        for i in parts:
            prevf[i].wait_recv()
        norms(PREV)
        norms(PREV + 1)

        @pl.when(jnp.logical_not(high_b))
        def _():
            rsum[PREV + c] += sweep(rows.at[PREV + c], 0, 4)

        for i in parts:
            xprev[i].wait_recv()
            xprevf[i].start()
        for i in parts:
            xprevf[i].wait_recv()
        norms(XPREV)
        norms(XPREV + 1)

        @pl.when(jnp.logical_or(first_a, high_a))
        def _():
            rsum[XPREV + c] += sweep(rows.at[XPREV + c], 0, 4)

    @pl.when(has_nxt)
    def _():
        for i in parts:
            nxtc[i].wait_recv()
        ncol[...] = sweep(nxt, 0, jnp.where(first_b, 4, 8))

    @pl.when(has_nxt2)
    def _():
        for i in parts:
            nxt2c[i].wait_recv()
        ncol2[...] = sweep(nxt2, jnp.where(first, 4, 0), 8)

    def gain(src, slot, device, ks):
        return copy(src, gains.at[slot], f_gain + slot, device, f_gain + ks)

    g_own = [gain(rsum.at[OWN + 1 - c], 0, core, 0)]
    g_own += [gain(rsum.at[CROSS + k], 1 + c, dev(0, 1 - h, k), 1 + k) for k in range(2)]
    g_prev = [gain(rsum.at[PREV + k], 3 + c, dev(-1, h, k), 3 + k) for k in range(2)]
    g_prev += [gain(rsum.at[XPREV + k], 5 + c, dev(-1, 1 - h, k), 5 + k) for k in range(2)]
    g_nxt = gain(ncol, 7, dev(2, h, c), 7)
    g_nxt2 = gain(ncol2, 8, dev(2, 1 - h, c), 8)

    pl.when(has_nxt)(g_nxt.start)
    pl.when(has_nxt2)(g_nxt2.start)

    @pl.when(has_prev)
    def _():
        for q in g_prev:
            q.start()

    for q in g_own:
        q.start()

    def arrive(slot):
        copy(gains.at[slot], gains.at[slot], f_gain + slot, core).wait_recv()
        rsum[OWN + c] += gains[slot]

    for slot in range(3):
        arrive(slot)

    @pl.when(jnp.logical_or(not_last, is_a))
    def _():
        arrive(3)
        arrive(4)

    @pl.when(jnp.logical_or(not_last, is_b))
    def _():
        arrive(5)
        arrive(6)

    pl.when(jnp.logical_not(low_a))(lambda: arrive(7))
    pl.when(send_nxt2)(lambda: arrive(8))

    out[...] = jnp.log1p(jnp.sum(rsum[OWN + c], axis=0, keepdims=True))

    own_copy.wait_send()
    for i in parts:
        cross[i].wait_send()
        crossf[i].wait_send()
        pl.when(not_last)(prev[i].wait_send)
        pl.when(last_b)(prev_relay[i].wait_send)
        pl.when(has_prev)(prevf[i].wait_send)
        pl.when(send_xprev)(xprev[i].wait_send)
        pl.when(has_prev)(xprevf[i].wait_send)
        pl.when(not_low)(nxtc[i].wait_send)
        pl.when(low_b)(nxt_relay[i].wait_send)
        pl.when(low_a)(to_relay[i].wait_send)
        pl.when(send_nxt2)(nxt2c[i].wait_send)
    for q in g_own:
        q.wait_send()

    @pl.when(has_prev)
    def _():
        for q in g_prev:
            q.wait_send()

    pl.when(has_nxt)(g_nxt.wait_send)
    pl.when(has_nxt2)(g_nxt2.wait_send)


def solution(mesh):
    n_blk = mesh.shape["blk"]

    def body(embeddings):
        block, width = embeddings.shape
        n_sem = 1 + 9 * CHUNKS + 10
        sums = pl.pallas_call(
            functools.partial(kernel, n_blk, block, width),
            out_shape=jax.ShapeDtypeStruct((1, block), jnp.float32),
            in_specs=[pl.BlockSpec(memory_space=pl.ANY)],
            out_specs=pl.BlockSpec(memory_space=pltpu.VMEM),
            scratch_shapes=[
                pltpu.VMEM((8, block, width), jnp.bfloat16),
                pltpu.VMEM((block, width), jnp.bfloat16),
                pltpu.VMEM((block, width), jnp.bfloat16),
                pltpu.VMEM((block, width), jnp.bfloat16),
                pltpu.VMEM((8, 8, block), jnp.float32),
                pltpu.VMEM((8, 8, block), jnp.float32),
                pltpu.VMEM((8, block), jnp.float32),
                pltpu.VMEM((8, block), jnp.float32),
                pltpu.VMEM((9, 8, block), jnp.float32),
                pltpu.SemaphoreType.DMA,
                pltpu.SemaphoreType.DMA((n_sem,)),
                pltpu.SemaphoreType.DMA((n_sem,)),
            ],
            compiler_params=pltpu.CompilerParams(
                collective_id=0, has_side_effects=True, vmem_limit_bytes=40 * 2**20
            ),
            cost_estimate=pl.CostEstimate(flops=2 * 16 * block * block * width, bytes_accessed=2 * block * width,
                                          transcendentals=16 * block * block),
        )(embeddings)
        return sums.reshape(block)

    return jax.shard_map(
        body, mesh=mesh, in_specs=(P(("blk", "grp"), None),), out_specs=P(("blk", "grp")), check_vma=False
    )
```

time: 382 us -> 76.5 us (0.20)
  waiting for transfers between devices: 323 us -> 0 us
  Pallas kernels: 0 us -> 74.2 us
  between operations: 14.2 us -> 0.01 us
  starting transfers between devices: 12.7 us -> 0 us
  blocking collectives: 11.1 us -> 0 us
  other arithmetic: 8.55 us -> 0 us
  matrix products: 7.24 us -> 0 us
    ppermute x6 -> x0, waiting for transfers between devices: 279 us -> none  [from_behind(): return lax.ppermute(block, axis, route)]
    pallas_call x0 -> x1, Pallas kernels: none -> 74.2 us  [body(): pl.pallas_call(functools.partial(kernel, n_blk, block, width), out_shape=...]
    all_gather x1 -> x0, waiting for transfers between devices: 42.8 us -> none  [body(): group_block = lax.all_gather(embeddings, 'grp', axis=0, tiled=True)]
    ppermute x6 -> x0, starting transfers between devices: 12.7 us -> none  [from_behind(): return lax.ppermute(block, axis, route)]
    unnamed x1 -> x0, blocking collectives: 11.1 us -> none
    dot_general x5 -> x0, other arithmetic: 7.96 us -> none  [squared_norms(): jnp.einsum('rd,rd->r', vectors, vectors, preferred_element_type=jnp.float32)]
    dot_general x4 -> x0, matrix products: 7.24 us -> none  [kernel_tile(): lax.dot_general(queries, targets, (((1,), (1,)), ((), ())), preferred_ele...]
  transfers between devices with their start and end apart: 7 -> 0, of which waited for: 6 -> 0; matrix products, arithmetic and copies ran while one was open for 3% -> 0% of each run, Pallas kernels for 0% -> 0%
where the time goes in v1:
time: 76.5 us; the launch traced here: 75.8 us
  Pallas kernels  74.2 us (97%)
  local copies, waits for them, and re-layouts  1.61 us (2%)
    pallas_call x1, Pallas kernels, body(): pl.pallas_call(functools.partial(kernel, n_blk, block, width), out_shape=...  74.2 us
    unnamed x3, local copies, waits for them, and re-layouts  1.61 us

profile of v1, /device:TPU:1, one launch (start us, length us, event | category | flops | bytes accessed | tf_op | source)
XLA Modules:
  0.0 75.8 jit_solution(15217992413222010964)
XLA Ops:
  0.0 0.0 copy-start
  0.0 1.0 %copy-done = bf16[256,1024]{1,0:T(8,128)(2,1)S(1)} copy-done((bf16[256,1024]{1,0:T(8,128)(2,1)S(1)}, bf16[256,1024]{1,0:T(8,128)(2,1)}, u32[]{:S(2)}) %copy-start) | copy-done | bytes 524312
  1.0 74.2 %shard_map.17 = f32[1,256]{1,0:T(1,128)S(1)} custom-call(bf16[256,1024]{1,0:T(8,128)(2,1)S(1)} %copy-done), custom_call_target="tpu_custom_call" | custom-call | flops 2147483648 | bytes 524288 | tf_op jit(solution)/shard_map/pallas_call | solution.py:306
  75.2 0.6 copy.3
Async XLA Ops:
  0.0 1.0 %copy-start = (bf16[256,1024]{1,0:T(8,128)(2,1)S(1)}, bf16[256,1024]{1,0:T(8,128)(2,1)}, u32[]{:S(2)}) copy-start(bf16[256,1024]{1,0:T(8,128)(2,1)} %x.1) | copy-start | bytes 1572868

commit v2 on v1

--- a/solution.py
+++ b/solution.py
@@ -13,15 +13,16 @@
 LOG2E = math.log2(math.e)
 SCALE = SHARPNESS * LOG2E
 CHUNKS = 4
+RELAYED = 3
 PERIOD = 32
 
 OWN, CROSS, PREV, XPREV = 0, 2, 4, 6
 
 
 def kernel(n_blk, block, width, x, out, rows, nxt, nxt2, relay, rsum, rnorm, ncol, ncol2, gains, lsem, ssem, rsem):
-    p = lax.axis_index("blk")
+    p = n_blk - 1 - lax.axis_index("blk")
     g = lax.axis_index("grp")
-    h = g // 2
+    h = 1 - g // 2
     c = lax.rem(g, 2)
     m = lax.rem(p, PERIOD)
     is_a, is_b = h == 0, h == 1
@@ -33,13 +34,13 @@
     low_a, low_b = jnp.logical_and(low, is_a), jnp.logical_and(low, is_b)
     high_a, high_b = jnp.logical_and(high, is_a), jnp.logical_and(high, is_b)
     last_b = jnp.logical_and(last, is_b)
-    send_xprev = jnp.logical_or(not_last, is_b)
-    send_nxt2 = jnp.logical_or(jnp.logical_and(m == 2, is_b), low_a)
+    inner = jnp.logical_not(first)
     first_a = jnp.logical_and(first, is_a)
     first_b = jnp.logical_and(first, is_b)
+    second_b = jnp.logical_and(m == 2, is_b)
 
     def dev(dp, hh, cc):
-        return (lax.rem(p + dp + n_blk, n_blk), hh * 2 + cc)
+        return (n_blk - 1 - lax.rem(p + dp + n_blk, n_blk), (1 - hh) * 2 + cc)
 
     step = block // CHUNKS
 
@@ -71,11 +72,14 @@
     prev = [copy(part(x, i), part(rows.at[PREV + c], i), f_prev + i, dev(1, h, c)) for i in parts]
     prev_relay = [copy(part(rows.at[CROSS + c], i), part(rows.at[PREV + c], i), f_prev + i, dev(1, 0, c)) for i in parts]
     prevf = [copy(part(rows.at[PREV + c], i), part(rows.at[PREV + c], i), f_prevf + i, core) for i in parts]
-    xprev = [copy(part(x, i), part(rows.at[XPREV + c], i), f_xprev + i, dev(1, 1 - h, c)) for i in parts]
+    xprev = [copy(part(rows.at[PREV + c], i), part(rows.at[XPREV + c], i), f_xprev + i, dev(0, 1 - h, c)) for i in parts]
+    xprev_own = [copy(part(x, i), part(rows.at[XPREV + c], i), f_xprev + i, dev(1, 0, c)) for i in parts]
     xprevf = [copy(part(rows.at[XPREV + c], i), part(rows.at[XPREV + c], i), f_xprevf + i, core) for i in parts]
     nxtc = [copy(part(x, i), part(nxt, i), f_nxt + i, dev(-2, h, c)) for i in parts]
-    nxt_relay = [copy(part(relay, i), part(nxt, i), f_nxt + i, dev(PERIOD - 2, 1, c)) for i in parts]
-    to_relay = [copy(part(rows.at[CROSS + c], i), part(relay, i), f_relay + i, dev(-PERIOD, 1, c)) for i in parts]
+    nxt_relay = [copy(part(relay, i), part(nxt, i), f_nxt + i, dev(PERIOD - 2, 1, c)) for i in parts[:RELAYED]]
+    to_relay = [copy(part(rows.at[CROSS + c], i), part(relay, i), f_relay + i, dev(-PERIOD, 1, c)) for i in parts[:RELAYED]]
+    to_relay += [copy(part(rows.at[CROSS + c], i), part(nxt, i), f_nxt + i, dev(-2, 1, c)) for i in parts[RELAYED:]]
+    nxt2_relay = [copy(part(nxt, i), part(nxt2, i), f_nxt2 + i, dev(0, 0, c)) for i in parts]
     nxt2c = [copy(part(x, i), part(nxt2, i), f_nxt2 + i, dev(-2, 1 - h, c)) for i in parts]
 
     local = pltpu.make_async_copy(x, rows.at[OWN + c], lsem)
@@ -89,27 +93,26 @@
     hello(core)
     hello(dev(0, 1 - h, c))
     pl.when(jnp.logical_not(first))(lambda: hello(dev(-1, h, c)))
-    pl.when(has_prev)(lambda: hello(dev(-1, 1 - h, c)))
+    pl.when(first_a)(lambda: hello(dev(-1, 1, c)))
     pl.when(jnp.logical_not(high))(lambda: hello(dev(2, h, c)))
     pl.when(high_b)(lambda: hello(dev(-(PERIOD - 2), 1, c)))
     pl.when(low_b)(lambda: hello(dev(PERIOD, 0, c)))
-    pl.when(has_nxt2)(lambda: hello(dev(2, 1 - h, c)))
+    pl.when(high_b)(lambda: hello(dev(2, 0, c)))
 
     def one(flag):
         return jnp.where(flag, 1, 0)
 
-    targets = 2 + one(not_last) + one(send_xprev) + 1 + one(send_nxt2)
+    targets = 2 + one(not_last) + one(last_b) + 1 + one(low_a)
     pl.semaphore_wait(barrier, targets)
 
     for i in parts:
         cross[i].start()
         pl.when(not_last)(prev[i].start)
         pl.when(not_low)(nxtc[i].start)
-        pl.when(send_nxt2)(nxt2c[i].start)
+        pl.when(low_a)(nxt2c[i].start)
+        pl.when(last_b)(xprev_own[i].start)
         if i == 0:
             own_copy.start()
-    for i in parts:
-        pl.when(send_xprev)(xprev[i].start)
 
     rsum[...] = jnp.zeros_like(rsum)
 
@@ -142,38 +145,40 @@
             total = total + e[:, k * 128:(k + 1) * 128]
         return total
 
-    def sweep(ref, lo, hi):
+    def sweep(target, target_norms, slots, acc):
+        for t in slots:
+            e = affinity(target, target_norms, t)
+            rsum[t] += jnp.sum(e.reshape(block // 8, 8, block), axis=0)
+            acc = acc + fold(e)
+        return acc
+
+    def whole(ref, slots):
         target = ref[...]
-        target_norms = column_norms(target)
-
-        def visit(s, acc):
-            e = affinity(target, target_norms, s)
-            rsum[s] += jnp.sum(e.reshape(block // 8, 8, block), axis=0)
-            return acc + fold(e)
-
-        acc = lax.fori_loop(lo, hi, visit, jnp.zeros((block, 128), jnp.float32))
-        return flat(acc, 0.125)
+        return flat(sweep(target, column_norms(target), slots, jnp.zeros((block, 128), jnp.float32)), 0.125)
 
     local.wait()
     norms(OWN + c)
 
+    def pass_relay(i):
+        to_relay[i].wait_recv()
+        nxt_relay[i].start()
+
+    def pass_prev(i):
+        prev[i].wait_recv()
+        prevf[i].start()
+
+    def pass_both(i):
+        pass_prev(i)
+        xprev[i].start()
+
     for i in parts:
         cross[i].wait_recv()
-        crossf[i].start()
         pl.when(low_a)(to_relay[i].start)
         pl.when(last_b)(prev_relay[i].start)
-
-    @pl.when(low_b)
-    def _():
-        for i in parts:
-            to_relay[i].wait_recv()
-            nxt_relay[i].start()
-
-    @pl.when(has_prev)
-    def _():
-        for i in parts:
-            prev[i].wait_recv()
-            prevf[i].start()
+        crossf[i].start()
+        pl.when(inner)(functools.partial(pass_both, i))
+        if i >= 1:
+            pl.when(low_b)(functools.partial(pass_relay, i - 1))
 
     own_copy.wait_recv()
     norms(OWN + 1 - c)
@@ -186,48 +191,94 @@
     mine_norms = column_norms(mine)
     diagonal = lax.broadcasted_iota(jnp.int32, (block, block), 0) == lax.broadcasted_iota(jnp.int32, (block, block), 1)
 
-    def visit_own(s, acc):
-        e = affinity(mine, mine_norms, s)
-        e = jnp.where(jnp.logical_and(diagonal, s == OWN + c), 0.0, e)
-        return acc + fold(e)
-
-    acc = lax.fori_loop(0, 4, visit_own, jnp.zeros((block, 128), jnp.float32))
+    acc = jnp.zeros((block, 128), jnp.float32)
+    for t in range(4):
+        e = affinity(mine, mine_norms, t)
+        if t < 2:
+            e = jnp.where(jnp.logical_and(diagonal, c == t), 0.0, e)
+        acc = acc + fold(e)
     rsum[OWN + c] += flat(acc, 0.125)
 
-    @pl.when(has_prev)
-    def _():
+    def get_prev():
         for i in parts:
             prevf[i].wait_recv()
         norms(PREV)
         norms(PREV + 1)
 
-        @pl.when(jnp.logical_not(high_b))
-        def _():
-            rsum[PREV + c] += sweep(rows.at[PREV + c], 0, 4)
-
-        for i in parts:
+    def pass_xprev(some):
+        for i in some:
             xprev[i].wait_recv()
             xprevf[i].start()
+
+    def get_xprev():
         for i in parts:
             xprevf[i].wait_recv()
         norms(XPREV)
         norms(XPREV + 1)
 
-        @pl.when(jnp.logical_or(first_a, high_a))
+    def get_nxt():
+        for i in parts:
+            nxtc[i].wait_recv()
+        target = nxt[...]
+        return target, column_norms(target), jnp.zeros((block, 128), jnp.float32)
+
+    @pl.when(inner)
+    def _():
+        get_prev()
+
+        @pl.when(jnp.logical_not(high_b))
         def _():
-            rsum[XPREV + c] += sweep(rows.at[XPREV + c], 0, 4)
-
-    @pl.when(has_nxt)
+            rsum[PREV + c] += whole(rows.at[PREV + c], range(4))
+
+    @pl.when(jnp.logical_and(inner, jnp.logical_not(high)))
+    def _():
+        pass_xprev(parts[:-1])
+        target, target_norms, acc = get_nxt()
+        acc = sweep(target, target_norms, range(4), acc)
+        pass_xprev(parts[-1:])
+        acc = sweep(target, target_norms, range(4, 6), acc)
+        get_xprev()
+        ncol[...] = flat(sweep(target, target_norms, range(6, 8), acc), 0.125)
+
+    @pl.when(first_b)
     def _():
         for i in parts:
             nxtc[i].wait_recv()
-        ncol[...] = sweep(nxt, 0, jnp.where(first_b, 4, 8))
-
-    @pl.when(has_nxt2)
-    def _():
+            nxt2_relay[i].start()
+        ncol[...] = whole(nxt, range(4))
+
+    @pl.when(first_a)
+    def _():
+        target, target_norms, acc = get_nxt()
+        acc = sweep(target, target_norms, range(4), acc)
+        pass_xprev(parts)
+        for i in parts:
+            pass_prev(i)
+        get_xprev()
+        rsum[XPREV + c] += whole(rows.at[XPREV + c], range(4))
+        acc = sweep(target, target_norms, range(6, 8), acc)
+        get_prev()
+        rsum[PREV + c] += whole(rows.at[PREV + c], range(4))
+        ncol[...] = flat(sweep(target, target_norms, range(4, 6), acc), 0.125)
         for i in parts:
             nxt2c[i].wait_recv()
-        ncol2[...] = sweep(nxt2, jnp.where(first, 4, 0), 8)
+        ncol2[...] = whole(nxt2, range(PREV, 8))
+
+    @pl.when(high_a)
+    def _():
+        pass_xprev(parts)
+        get_xprev()
+        rsum[XPREV + c] += whole(rows.at[XPREV + c], range(4))
+
+    @pl.when(high_b)
+    def _():
+        pass_xprev(parts)
+        get_xprev()
+        for i in parts:
+            nxt2c[i].wait_recv()
+        ncol2[...] = whole(nxt2, range(8))
+        target, target_norms, acc = get_nxt()
+        ncol[...] = flat(sweep(target, target_norms, range(8), acc), 0.125)
 
     def gain(src, slot, device, ks):
         return copy(src, gains.at[slot], f_gain + slot, device, f_gain + ks)
@@ -268,7 +319,7 @@
         arrive(6)
 
     pl.when(jnp.logical_not(low_a))(lambda: arrive(7))
-    pl.when(send_nxt2)(lambda: arrive(8))
+    pl.when(jnp.logical_or(low_a, second_b))(lambda: arrive(8))
 
     out[...] = jnp.log1p(jnp.sum(rsum[OWN + c], axis=0, keepdims=True))
 
@@ -279,12 +330,15 @@
         pl.when(not_last)(prev[i].wait_send)
         pl.when(last_b)(prev_relay[i].wait_send)
         pl.when(has_prev)(prevf[i].wait_send)
-        pl.when(send_xprev)(xprev[i].wait_send)
+        pl.when(inner)(xprev[i].wait_send)
+        pl.when(last_b)(xprev_own[i].wait_send)
         pl.when(has_prev)(xprevf[i].wait_send)
         pl.when(not_low)(nxtc[i].wait_send)
-        pl.when(low_b)(nxt_relay[i].wait_send)
+        if i < RELAYED:
+            pl.when(low_b)(nxt_relay[i].wait_send)
         pl.when(low_a)(to_relay[i].wait_send)
-        pl.when(send_nxt2)(nxt2c[i].wait_send)
+        pl.when(low_a)(nxt2c[i].wait_send)
+        pl.when(first_b)(nxt2_relay[i].wait_send)
     for q in g_own:
         q.wait_send()
 

time: 76.5 us -> 56.3 us (0.74)
  Pallas kernels: 74.2 us -> 54.5 us
    pallas_call x1, Pallas kernels: 74.2 us -> 54.5 us  [body(): pl.pallas_call(functools.partial(kernel, n_blk, block, width), out_shape=...]
where the time goes in v2:
time: 56.3 us; the launch traced here: 56.1 us
  Pallas kernels  54.5 us (97%)
  local copies, waits for them, and re-layouts  1.61 us (3%)
    pallas_call x1, Pallas kernels, body(): pl.pallas_call(functools.partial(kernel, n_blk, block, width), out_shape=...  54.5 us
    unnamed x3, local copies, waits for them, and re-layouts  1.61 us

profile of v2, /device:TPU:1, one launch (start us, length us, event | category | flops | bytes accessed | tf_op | source)
XLA Modules:
  0.0 56.1 jit_solution(12536947471137203607)
XLA Ops:
  0.0 0.0 copy-start
  0.0 1.0 %copy-done = bf16[256,1024]{1,0:T(8,128)(2,1)S(1)} copy-done((bf16[256,1024]{1,0:T(8,128)(2,1)S(1)}, bf16[256,1024]{1,0:T(8,128)(2,1)}, u32[]{:S(2)}) %copy-start) | copy-done | bytes 524312
  1.0 54.5 %shard_map.17 = f32[1,256]{1,0:T(1,128)S(1)} custom-call(bf16[256,1024]{1,0:T(8,128)(2,1)S(1)} %copy-done), custom_call_target="tpu_custom_call" | custom-call | flops 2147483648 | bytes 524288 | tf_op jit(solution)/shard_map/pallas_call | solution.py:360
  55.5 0.6 %copy.3 = f32[256]{0:T(256)} copy(f32[256]{0:T(256)S(1)} %bitcast.1) | data formatting | bytes 2048
Async XLA Ops:
  0.0 1.0 %copy-start = (bf16[256,1024]{1,0:T(8,128)(2,1)S(1)}, bf16[256,1024]{1,0:T(8,128)(2,1)}, u32[]{:S(2)}) copy-start(bf16[256,1024]{1,0:T(8,128)(2,1)} %x.1) | copy-start | bytes 1572868

commit v3 on v2

--- a/solution.py
+++ b/solution.py
@@ -13,8 +13,9 @@
 LOG2E = math.log2(math.e)
 SCALE = SHARPNESS * LOG2E
 CHUNKS = 4
-RELAYED = 3
+PREV_CUT, XPREV_CUT, NXT_CUT = 0, 2, 2
 PERIOD = 32
+ROW = 8
 
 OWN, CROSS, PREV, XPREV = 0, 2, 4, 6
 
@@ -31,9 +32,10 @@
     has_nxt = jnp.logical_not(jnp.logical_and(high, is_a))
     has_nxt2 = jnp.logical_or(jnp.logical_and(first, is_a), jnp.logical_and(high, is_b))
     not_last, not_low = jnp.logical_not(last), jnp.logical_not(low)
+    turn_a = jnp.logical_and(m == ROW - 1, is_a)
     low_a, low_b = jnp.logical_and(low, is_a), jnp.logical_and(low, is_b)
     high_a, high_b = jnp.logical_and(high, is_a), jnp.logical_and(high, is_b)
-    last_b = jnp.logical_and(last, is_b)
+    last_a, last_b = jnp.logical_and(last, is_a), jnp.logical_and(last, is_b)
     inner = jnp.logical_not(first)
     first_a = jnp.logical_and(first, is_a)
     first_b = jnp.logical_and(first, is_b)
@@ -63,6 +65,7 @@
     f_cross, f_crossf, f_prev, f_prevf = flow(CHUNKS), flow(CHUNKS), flow(CHUNKS), flow(CHUNKS)
     f_xprev, f_xprevf, f_nxt, f_nxt2, f_relay = flow(CHUNKS), flow(CHUNKS), flow(CHUNKS), flow(CHUNKS), flow(CHUNKS)
     f_gain = flow(10)
+    f_far = flow(CHUNKS)
 
     core = dev(0, h, 1 - c)
     parts = range(CHUNKS)
@@ -76,9 +79,10 @@
     xprev_own = [copy(part(x, i), part(rows.at[XPREV + c], i), f_xprev + i, dev(1, 0, c)) for i in parts]
     xprevf = [copy(part(rows.at[XPREV + c], i), part(rows.at[XPREV + c], i), f_xprevf + i, core) for i in parts]
     nxtc = [copy(part(x, i), part(nxt, i), f_nxt + i, dev(-2, h, c)) for i in parts]
-    nxt_relay = [copy(part(relay, i), part(nxt, i), f_nxt + i, dev(PERIOD - 2, 1, c)) for i in parts[:RELAYED]]
-    to_relay = [copy(part(rows.at[CROSS + c], i), part(relay, i), f_relay + i, dev(-PERIOD, 1, c)) for i in parts[:RELAYED]]
-    to_relay += [copy(part(rows.at[CROSS + c], i), part(nxt, i), f_nxt + i, dev(-2, 1, c)) for i in parts[RELAYED:]]
+    to_relay = [copy(part(rows.at[CROSS + c], i), part(relay, i), f_relay + i, dev(-PERIOD, 1, c)) for i in parts[:NXT_CUT]]
+    nxt_relay = [copy(part(relay, i), part(nxt, i), f_nxt + i, dev(PERIOD - 2, 1, c)) for i in parts[:NXT_CUT]]
+    to_far = [copy(part(x, i), part(relay, i), f_relay + i, dev(ROW, 0, c)) for i in parts]
+    far = [copy(part(relay, i), part(rows.at[XPREV + c], i), f_xprev + i, dev(1 - ROW, 0, c), f_far + i) for i in parts]
     nxt2_relay = [copy(part(nxt, i), part(nxt2, i), f_nxt2 + i, dev(0, 0, c)) for i in parts]
     nxt2c = [copy(part(x, i), part(nxt2, i), f_nxt2 + i, dev(-2, 1 - h, c)) for i in parts]
 
@@ -92,25 +96,40 @@
 
     hello(core)
     hello(dev(0, 1 - h, c))
-    pl.when(jnp.logical_not(first))(lambda: hello(dev(-1, h, c)))
-    pl.when(first_a)(lambda: hello(dev(-1, 1, c)))
-    pl.when(jnp.logical_not(high))(lambda: hello(dev(2, h, c)))
-    pl.when(high_b)(lambda: hello(dev(-(PERIOD - 2), 1, c)))
+    pl.when(has_prev)(lambda: hello(dev(-1, h, c)))
+    pl.when(has_nxt)(lambda: hello(dev(2, h, c)))
+
+    @pl.when(first_a)
+    def _():
+        hello(dev(-1, 1, c))
+        hello(dev(ROW - 1, 0, c))
+
+    @pl.when(high_b)
+    def _():
+        hello(dev(2, 0, c))
+        hello(dev(2 - PERIOD, 1, c))
+
+    pl.when(turn_a)(lambda: hello(dev(-ROW, 1, c)))
     pl.when(low_b)(lambda: hello(dev(PERIOD, 0, c)))
-    pl.when(high_b)(lambda: hello(dev(2, 0, c)))
 
     def one(flag):
         return jnp.where(flag, 1, 0)
 
-    targets = 2 + one(not_last) + one(last_b) + 1 + one(low_a)
+    targets = 4 + one(last_b) + one(turn_a) + one(low)
     pl.semaphore_wait(barrier, targets)
+
+    def sends_prev(i):
+        return not_last if i < PREV_CUT else jnp.logical_or(not_last, is_a)
+
+    def sends_nxt(i):
+        return not_low if i < NXT_CUT else jnp.logical_or(not_low, is_b)
 
     for i in parts:
         cross[i].start()
-        pl.when(not_last)(prev[i].start)
-        pl.when(not_low)(nxtc[i].start)
+        pl.when(sends_prev(i))(prev[i].start)
+        pl.when(sends_nxt(i))(nxtc[i].start)
+        pl.when(last_b)(xprev_own[i].start if i < XPREV_CUT else to_far[i].start)
         pl.when(low_a)(nxt2c[i].start)
-        pl.when(last_b)(xprev_own[i].start)
         if i == 0:
             own_copy.start()
 
@@ -124,13 +143,12 @@
             total = total + v[:, k * 128:(k + 1) * 128]
         return total
 
-    def flat(acc, weight):
-        ones = jnp.full((8, 128), weight, jnp.float32)
-        return lax.dot_general(ones, acc, (((1,), (1,)), ((), ())), precision=lax.Precision.HIGHEST,
-                               preferred_element_type=jnp.float32)
+    def flat(acc):
+        return jnp.sum(acc.T.reshape(16, 8, block), axis=0)
 
     def norms(s):
-        rnorm[s] = flat(squares(rows[s]), 1.0) * SCALE
+        total = jnp.sum(flat(squares(rows[s])), axis=0, keepdims=True) * SCALE
+        rnorm[s] = jnp.broadcast_to(total, (8, block))
 
     def column_norms(block_rows):
         return jnp.sum(squares(block_rows), axis=1, keepdims=True) * SCALE
@@ -154,7 +172,7 @@
 
     def whole(ref, slots):
         target = ref[...]
-        return flat(sweep(target, column_norms(target), slots, jnp.zeros((block, 128), jnp.float32)), 0.125)
+        return flat(sweep(target, column_norms(target), slots, jnp.zeros((block, 128), jnp.float32)))
 
     local.wait()
     norms(OWN + c)
@@ -163,6 +181,10 @@
         to_relay[i].wait_recv()
         nxt_relay[i].start()
 
+    def pass_far(i):
+        to_far[i].wait_recv()
+        far[i].start()
+
     def pass_prev(i):
         prev[i].wait_recv()
         prevf[i].start()
@@ -173,12 +195,16 @@
 
     for i in parts:
         cross[i].wait_recv()
-        pl.when(low_a)(to_relay[i].start)
-        pl.when(last_b)(prev_relay[i].start)
+        if i < NXT_CUT:
+            pl.when(low_a)(to_relay[i].start)
+        if i < PREV_CUT:
+            pl.when(last_b)(prev_relay[i].start)
         crossf[i].start()
         pl.when(inner)(functools.partial(pass_both, i))
-        if i >= 1:
+        if 1 <= i <= NXT_CUT:
             pl.when(low_b)(functools.partial(pass_relay, i - 1))
+        if i >= XPREV_CUT:
+            pl.when(turn_a)(functools.partial(pass_far, i))
 
     own_copy.wait_recv()
     norms(OWN + 1 - c)
@@ -197,7 +223,7 @@
         if t < 2:
             e = jnp.where(jnp.logical_and(diagonal, c == t), 0.0, e)
         acc = acc + fold(e)
-    rsum[OWN + c] += flat(acc, 0.125)
+    rsum[OWN + c] += flat(acc)
 
     def get_prev():
         for i in parts:
@@ -238,7 +264,7 @@
         pass_xprev(parts[-1:])
         acc = sweep(target, target_norms, range(4, 6), acc)
         get_xprev()
-        ncol[...] = flat(sweep(target, target_norms, range(6, 8), acc), 0.125)
+        ncol[...] = flat(sweep(target, target_norms, range(6, 8), acc))
 
     @pl.when(first_b)
     def _():
@@ -247,22 +273,53 @@
             nxt2_relay[i].start()
         ncol[...] = whole(nxt, range(4))
 
+    def gain(src, slot, device, ks):
+        return copy(src, gains.at[slot], f_gain + slot, device, f_gain + ks)
+
+    g_own = [gain(rsum.at[OWN + 1 - c], 0, core, 0)]
+    g_own += [gain(rsum.at[CROSS + k], 1 + c, dev(0, 1 - h, k), 1 + k) for k in range(2)]
+    g_prev = [gain(rsum.at[PREV + k], 3 + c, dev(-1, h, k), 3 + k) for k in range(2)]
+    g_xprev = [gain(rsum.at[XPREV + k], 5 + c, dev(-1, 1 - h, k), 5 + k) for k in range(2)]
+    g_nxt = gain(ncol, 7, dev(2, h, c), 7)
+    g_nxt2 = gain(ncol2, 8, dev(2, 1 - h, c), 8)
+
     @pl.when(first_a)
     def _():
+        for i in parts[:-1]:
+            pass_xprev([i])
+            pass_prev(i)
         target, target_norms, acc = get_nxt()
         acc = sweep(target, target_norms, range(4), acc)
-        pass_xprev(parts)
-        for i in parts:
-            pass_prev(i)
+        other = rows[CROSS + c]
+        other_norms = column_norms(other)
+        for i in parts:
+            nxt2c[i].wait_recv()
+        target2 = nxt2[...]
+        target2_norms = column_norms(target2)
+        pass_xprev(parts[-1:])
+        pass_prev(parts[-1])
+        zero = jnp.zeros((block, 128), jnp.float32)
+        accs = [zero, zero, acc, zero]
+
+        def against(slots):
+            for t in slots:
+                accs[0] = sweep(mine, mine_norms, [t], accs[0])
+                accs[1] = sweep(other, other_norms, [t], accs[1])
+                accs[2] = sweep(target, target_norms, [t], accs[2])
+                accs[3] = sweep(target2, target2_norms, [t], accs[3])
+
         get_xprev()
-        rsum[XPREV + c] += whole(rows.at[XPREV + c], range(4))
-        acc = sweep(target, target_norms, range(6, 8), acc)
+        against(range(XPREV, XPREV + 2))
+        for q in g_xprev:
+            q.start()
         get_prev()
-        rsum[PREV + c] += whole(rows.at[PREV + c], range(4))
-        ncol[...] = flat(sweep(target, target_norms, range(4, 6), acc), 0.125)
-        for i in parts:
-            nxt2c[i].wait_recv()
-        ncol2[...] = whole(nxt2, range(PREV, 8))
+        against(range(PREV, PREV + 2))
+        for q in g_prev:
+            q.start()
+        rsum[OWN + c] += flat(accs[0])
+        rsum[CROSS + c] += flat(accs[1])
+        ncol[...] = flat(accs[2])
+        ncol2[...] = flat(accs[3])
 
     @pl.when(high_a)
     def _():
@@ -278,28 +335,18 @@
             nxt2c[i].wait_recv()
         ncol2[...] = whole(nxt2, range(8))
         target, target_norms, acc = get_nxt()
-        ncol[...] = flat(sweep(target, target_norms, range(8), acc), 0.125)
-
-    def gain(src, slot, device, ks):
-        return copy(src, gains.at[slot], f_gain + slot, device, f_gain + ks)
-
-    g_own = [gain(rsum.at[OWN + 1 - c], 0, core, 0)]
-    g_own += [gain(rsum.at[CROSS + k], 1 + c, dev(0, 1 - h, k), 1 + k) for k in range(2)]
-    g_prev = [gain(rsum.at[PREV + k], 3 + c, dev(-1, h, k), 3 + k) for k in range(2)]
-    g_prev += [gain(rsum.at[XPREV + k], 5 + c, dev(-1, 1 - h, k), 5 + k) for k in range(2)]
-    g_nxt = gain(ncol, 7, dev(2, h, c), 7)
-    g_nxt2 = gain(ncol2, 8, dev(2, 1 - h, c), 8)
+        ncol[...] = flat(sweep(target, target_norms, range(8), acc))
+
+    @pl.when(inner)
+    def _():
+        for q in g_xprev + g_prev:
+            q.start()
+
+    for q in g_own:
+        q.start()
 
     pl.when(has_nxt)(g_nxt.start)
     pl.when(has_nxt2)(g_nxt2.start)
-
-    @pl.when(has_prev)
-    def _():
-        for q in g_prev:
-            q.start()
-
-    for q in g_own:
-        q.start()
 
     def arrive(slot):
         copy(gains.at[slot], gains.at[slot], f_gain + slot, core).wait_recv()
@@ -327,24 +374,29 @@
     for i in parts:
         cross[i].wait_send()
         crossf[i].wait_send()
-        pl.when(not_last)(prev[i].wait_send)
-        pl.when(last_b)(prev_relay[i].wait_send)
         pl.when(has_prev)(prevf[i].wait_send)
+        pl.when(has_prev)(xprevf[i].wait_send)
         pl.when(inner)(xprev[i].wait_send)
-        pl.when(last_b)(xprev_own[i].wait_send)
-        pl.when(has_prev)(xprevf[i].wait_send)
-        pl.when(not_low)(nxtc[i].wait_send)
-        if i < RELAYED:
-            pl.when(low_b)(nxt_relay[i].wait_send)
-        pl.when(low_a)(to_relay[i].wait_send)
         pl.when(low_a)(nxt2c[i].wait_send)
         pl.when(first_b)(nxt2_relay[i].wait_send)
+        pl.when(sends_prev(i))(prev[i].wait_send)
+        pl.when(sends_nxt(i))(nxtc[i].wait_send)
+        if i < PREV_CUT:
+            pl.when(last_b)(prev_relay[i].wait_send)
+        if i < XPREV_CUT:
+            pl.when(last_b)(xprev_own[i].wait_send)
+        else:
+            pl.when(last_b)(to_far[i].wait_send)
+            pl.when(turn_a)(far[i].wait_send)
+        if i < NXT_CUT:
+            pl.when(low_b)(nxt_relay[i].wait_send)
+            pl.when(low_a)(to_relay[i].wait_send)
     for q in g_own:
         q.wait_send()
 
     @pl.when(has_prev)
     def _():
-        for q in g_prev:
+        for q in g_xprev + g_prev:
             q.wait_send()
 
     pl.when(has_nxt)(g_nxt.wait_send)
@@ -356,7 +408,7 @@
 
     def body(embeddings):
         block, width = embeddings.shape
-        n_sem = 1 + 9 * CHUNKS + 10
+        n_sem = 1 + 10 * CHUNKS + 10
         sums = pl.pallas_call(
             functools.partial(kernel, n_blk, block, width),
             out_shape=jax.ShapeDtypeStruct((1, block), jnp.float32),

time: 56.3 us -> 52.8 us (0.938)
  Pallas kernels: 54.5 us -> 51 us
    pallas_call x1, Pallas kernels: 54.5 us -> 51 us  [body(): pl.pallas_call(functools.partial(kernel, n_blk, block, width), out_shape=...]
where the time goes in v3:
time: 52.8 us; the launch traced here: 52.6 us
  Pallas kernels  51 us (97%)
  local copies, waits for them, and re-layouts  1.61 us (3%)
    pallas_call x1, Pallas kernels, body(): pl.pallas_call(functools.partial(kernel, n_blk, block, width), out_shape=...  51 us
    unnamed x3, local copies, waits for them, and re-layouts  1.61 us

profile of v3, /device:TPU:1, one launch (start us, length us, event | category | flops | bytes accessed | tf_op | source)
XLA Modules:
  0.0 52.6 jit_solution(4751224563371766228)
XLA Ops:
  0.0 0.0 copy-start
  0.0 1.0 %copy-done = bf16[256,1024]{1,0:T(8,128)(2,1)S(1)} copy-done((bf16[256,1024]{1,0:T(8,128)(2,1)S(1)}, bf16[256,1024]{1,0:T(8,128)(2,1)}, u32[]{:S(2)}) %copy-start) | copy-done | bytes 524312
  1.0 51.0 %shard_map.17 = f32[1,256]{1,0:T(1,128)S(1)} custom-call(bf16[256,1024]{1,0:T(8,128)(2,1)S(1)} %copy-done), custom_call_target="tpu_custom_call" | custom-call | flops 2147483648 | bytes 524288 | tf_op jit(solution)/shard_map/pallas_call | solution.py:412
  52.1 0.6 %copy.3 = f32[256]{0:T(256)} copy(f32[256]{0:T(256)S(1)} %bitcast.1) | data formatting | bytes 2048
Async XLA Ops:
  0.0 1.0 %copy-start = (bf16[256,1024]{1,0:T(8,128)(2,1)S(1)}, bf16[256,1024]{1,0:T(8,128)(2,1)}, u32[]{:S(2)}) copy-start(bf16[256,1024]{1,0:T(8,128)(2,1)} %x.1) | copy-start | bytes 1572868

commit v4 on v3

--- a/solution.py
+++ b/solution.py
@@ -13,7 +13,7 @@
 LOG2E = math.log2(math.e)
 SCALE = SHARPNESS * LOG2E
 CHUNKS = 4
-PREV_CUT, XPREV_CUT, NXT_CUT = 0, 2, 2
+PREV_CUT, NXT_CUT, NXT2_CUT = 3, 2, 4
 PERIOD = 32
 ROW = 8
 
@@ -83,7 +83,12 @@
     nxt_relay = [copy(part(relay, i), part(nxt, i), f_nxt + i, dev(PERIOD - 2, 1, c)) for i in parts[:NXT_CUT]]
     to_far = [copy(part(x, i), part(relay, i), f_relay + i, dev(ROW, 0, c)) for i in parts]
     far = [copy(part(relay, i), part(rows.at[XPREV + c], i), f_xprev + i, dev(1 - ROW, 0, c), f_far + i) for i in parts]
+    to_far_prev = [copy(part(rows.at[CROSS + c], i), part(relay, i - PREV_CUT), f_relay + i - PREV_CUT, dev(ROW, 0, c))
+                   if i >= PREV_CUT else None for i in parts]
+    far_prev = [copy(part(relay, i - PREV_CUT), part(rows.at[PREV + c], i), f_prev + i, dev(1 - ROW, 0, c), f_far + i - PREV_CUT)
+                if i >= PREV_CUT else None for i in parts]
     nxt2_relay = [copy(part(nxt, i), part(nxt2, i), f_nxt2 + i, dev(0, 0, c)) for i in parts]
+    nxt2_cross = [copy(part(rows.at[CROSS + c], i), part(nxt2, i), f_nxt2 + i, dev(-2, 1, c)) for i in parts]
     nxt2c = [copy(part(x, i), part(nxt2, i), f_nxt2 + i, dev(-2, 1 - h, c)) for i in parts]
 
     local = pltpu.make_async_copy(x, rows.at[OWN + c], lsem)
@@ -96,7 +101,7 @@
 
     hello(core)
     hello(dev(0, 1 - h, c))
-    pl.when(has_prev)(lambda: hello(dev(-1, h, c)))
+    pl.when(inner)(lambda: hello(dev(-1, h, c)))
     pl.when(has_nxt)(lambda: hello(dev(2, h, c)))
 
     @pl.when(first_a)
@@ -115,21 +120,19 @@
     def one(flag):
         return jnp.where(flag, 1, 0)
 
-    targets = 4 + one(last_b) + one(turn_a) + one(low)
+    targets = 3 + one(not_last) + 2 * one(last_b) + one(turn_a) + one(low)
     pl.semaphore_wait(barrier, targets)
-
-    def sends_prev(i):
-        return not_last if i < PREV_CUT else jnp.logical_or(not_last, is_a)
 
     def sends_nxt(i):
         return not_low if i < NXT_CUT else jnp.logical_or(not_low, is_b)
 
     for i in parts:
         cross[i].start()
-        pl.when(sends_prev(i))(prev[i].start)
+        pl.when(not_last)(prev[i].start)
         pl.when(sends_nxt(i))(nxtc[i].start)
-        pl.when(last_b)(xprev_own[i].start if i < XPREV_CUT else to_far[i].start)
-        pl.when(low_a)(nxt2c[i].start)
+        pl.when(last_b)(xprev_own[i].start if i < PREV_CUT else to_far[i].start)
+        if i < NXT2_CUT:
+            pl.when(low_a)(nxt2c[i].start)
         if i == 0:
             own_copy.start()
 
@@ -184,6 +187,8 @@
     def pass_far(i):
         to_far[i].wait_recv()
         far[i].start()
+        to_far_prev[i].wait_recv()
+        far_prev[i].start()
 
     def pass_prev(i):
         prev[i].wait_recv()
@@ -192,18 +197,24 @@
     def pass_both(i):
         pass_prev(i)
         xprev[i].start()
+
+    @pl.when(last_a)
+    def _():
+        for i in parts:
+            pass_both(i)
 
     for i in parts:
         cross[i].wait_recv()
         if i < NXT_CUT:
             pl.when(low_a)(to_relay[i].start)
-        if i < PREV_CUT:
-            pl.when(last_b)(prev_relay[i].start)
+        if i >= NXT2_CUT:
+            pl.when(low_b)(nxt2_cross[i].start)
+        pl.when(last_b)(prev_relay[i].start if i < PREV_CUT else to_far_prev[i].start)
         crossf[i].start()
-        pl.when(inner)(functools.partial(pass_both, i))
+        pl.when(jnp.logical_and(inner, jnp.logical_not(last_a)))(functools.partial(pass_both, i))
         if 1 <= i <= NXT_CUT:
             pl.when(low_b)(functools.partial(pass_relay, i - 1))
-        if i >= XPREV_CUT:
+        if i >= PREV_CUT:
             pl.when(turn_a)(functools.partial(pass_far, i))
 
     own_copy.wait_recv()
@@ -288,54 +299,52 @@
         for i in parts[:-1]:
             pass_xprev([i])
             pass_prev(i)
-        target, target_norms, acc = get_nxt()
-        acc = sweep(target, target_norms, range(4), acc)
         other = rows[CROSS + c]
         other_norms = column_norms(other)
+        pass_xprev(parts[-1:])
+        pass_prev(parts[-1])
+        zero = jnp.zeros((block, 128), jnp.float32)
+        mine_acc, other_acc = zero, zero
+        get_xprev()
+        mine_acc = sweep(mine, mine_norms, range(XPREV, 8), mine_acc)
+        other_acc = sweep(other, other_norms, range(XPREV, 8), other_acc)
+        get_prev()
+        mine_acc = sweep(mine, mine_norms, range(PREV, XPREV), mine_acc)
+        other_acc = sweep(other, other_norms, range(PREV, XPREV), other_acc)
+        target, target_norms, acc = get_nxt()
+        acc = sweep(target, target_norms, range(PREV, 8), acc)
+        for i in parts:
+            nxt2c[i].wait_recv()
+        target2 = nxt2[...]
+        acc2 = sweep(target2, column_norms(target2), range(PREV, 8), zero)
+        for q in g_xprev:
+            q.start()
+        for q in g_prev:
+            q.start()
+        rsum[OWN + c] += flat(mine_acc)
+        rsum[CROSS + c] += flat(other_acc)
+        ncol[...] = flat(sweep(target, target_norms, range(4), acc))
+        ncol2[...] = flat(acc2)
+
+    @pl.when(high_a)
+    def _():
+        pass_xprev(parts)
+        get_xprev()
+        rsum[XPREV + c] += whole(rows.at[XPREV + c], range(4))
+
+    @pl.when(high_b)
+    def _():
+        pass_xprev(parts)
         for i in parts:
             nxt2c[i].wait_recv()
         target2 = nxt2[...]
         target2_norms = column_norms(target2)
-        pass_xprev(parts[-1:])
-        pass_prev(parts[-1])
-        zero = jnp.zeros((block, 128), jnp.float32)
-        accs = [zero, zero, acc, zero]
-
-        def against(slots):
-            for t in slots:
-                accs[0] = sweep(mine, mine_norms, [t], accs[0])
-                accs[1] = sweep(other, other_norms, [t], accs[1])
-                accs[2] = sweep(target, target_norms, [t], accs[2])
-                accs[3] = sweep(target2, target2_norms, [t], accs[3])
-
+        acc2 = sweep(target2, target2_norms, range(XPREV), jnp.zeros((block, 128), jnp.float32))
+        target, target_norms, acc = get_nxt()
+        acc = sweep(target, target_norms, range(XPREV), acc)
         get_xprev()
-        against(range(XPREV, XPREV + 2))
-        for q in g_xprev:
-            q.start()
-        get_prev()
-        against(range(PREV, PREV + 2))
-        for q in g_prev:
-            q.start()
-        rsum[OWN + c] += flat(accs[0])
-        rsum[CROSS + c] += flat(accs[1])
-        ncol[...] = flat(accs[2])
-        ncol2[...] = flat(accs[3])
-
-    @pl.when(high_a)
-    def _():
-        pass_xprev(parts)
-        get_xprev()
-        rsum[XPREV + c] += whole(rows.at[XPREV + c], range(4))
-
-    @pl.when(high_b)
-    def _():
-        pass_xprev(parts)
-        get_xprev()
-        for i in parts:
-            nxt2c[i].wait_recv()
-        ncol2[...] = whole(nxt2, range(8))
-        target, target_norms, acc = get_nxt()
-        ncol[...] = flat(sweep(target, target_norms, range(8), acc))
+        ncol2[...] = flat(sweep(target2, target2_norms, range(XPREV, 8), acc2))
+        ncol[...] = flat(sweep(target, target_norms, range(XPREV, 8), acc))
 
     @pl.when(inner)
     def _():
@@ -377,17 +386,21 @@
         pl.when(has_prev)(prevf[i].wait_send)
         pl.when(has_prev)(xprevf[i].wait_send)
         pl.when(inner)(xprev[i].wait_send)
-        pl.when(low_a)(nxt2c[i].wait_send)
+        if i < NXT2_CUT:
+            pl.when(low_a)(nxt2c[i].wait_send)
+        else:
+            pl.when(low_b)(nxt2_cross[i].wait_send)
         pl.when(first_b)(nxt2_relay[i].wait_send)
-        pl.when(sends_prev(i))(prev[i].wait_send)
+        pl.when(not_last)(prev[i].wait_send)
         pl.when(sends_nxt(i))(nxtc[i].wait_send)
         if i < PREV_CUT:
             pl.when(last_b)(prev_relay[i].wait_send)
-        if i < XPREV_CUT:
             pl.when(last_b)(xprev_own[i].wait_send)
         else:
             pl.when(last_b)(to_far[i].wait_send)
+            pl.when(last_b)(to_far_prev[i].wait_send)
             pl.when(turn_a)(far[i].wait_send)
+            pl.when(turn_a)(far_prev[i].wait_send)
         if i < NXT_CUT:
             pl.when(low_b)(nxt_relay[i].wait_send)
             pl.when(low_a)(to_relay[i].wait_send)

time: 52.8 us -> 51.3 us (0.972)
  Pallas kernels: 51 us -> 49.5 us
    pallas_call x1, Pallas kernels: 51 us -> 49.5 us  [body(): pl.pallas_call(functools.partial(kernel, n_blk, block, width), out_shape=...]
where the time goes in v4:
time: 51.3 us; the launch traced here: 51.1 us
  Pallas kernels  49.5 us (96%)
  local copies, waits for them, and re-layouts  1.61 us (3%)
    pallas_call x1, Pallas kernels, body(): pl.pallas_call(functools.partial(kernel, n_blk, block, width), out_shape=...  49.5 us
    unnamed x3, local copies, waits for them, and re-layouts  1.61 us

profile of v4, /device:TPU:1, one launch (start us, length us, event | category | flops | bytes accessed | tf_op | source)
XLA Modules:
  0.0 51.1 jit_solution(4522774447959068695)
XLA Ops:
  0.0 0.0 copy-start
  0.0 1.0 %copy-done = bf16[256,1024]{1,0:T(8,128)(2,1)S(1)} copy-done((bf16[256,1024]{1,0:T(8,128)(2,1)S(1)}, bf16[256,1024]{1,0:T(8,128)(2,1)}, u32[]{:S(2)}) %copy-start) | copy-done | bytes 524312
  1.0 49.5 %shard_map.17 = f32[1,256]{1,0:T(1,128)S(1)} custom-call(bf16[256,1024]{1,0:T(8,128)(2,1)S(1)} %copy-done), custom_call_target="tpu_custom_call" | custom-call | flops 2147483648 | bytes 524288 | tf_op jit(solution)/shard_map/pallas_call | solution.py:425
  50.5 0.6 %copy.3 = f32[256]{0:T(256)} copy(f32[256]{0:T(256)S(1)} %bitcast.1) | data formatting | bytes 2048
Async XLA Ops:
  0.0 1.0 %copy-start = (bf16[256,1024]{1,0:T(8,128)(2,1)S(1)}, bf16[256,1024]{1,0:T(8,128)(2,1)}, u32[]{:S(2)}) copy-start(bf16[256,1024]{1,0:T(8,128)(2,1)} %x.1) | copy-start | bytes 1572868

commit v5 on v4

--- a/solution.py
+++ b/solution.py
@@ -312,13 +312,16 @@
         mine_acc = sweep(mine, mine_norms, range(PREV, XPREV), mine_acc)
         other_acc = sweep(other, other_norms, range(PREV, XPREV), other_acc)
         target, target_norms, acc = get_nxt()
-        acc = sweep(target, target_norms, range(PREV, 8), acc)
+        acc = sweep(target, target_norms, range(XPREV, 8), acc)
         for i in parts:
             nxt2c[i].wait_recv()
         target2 = nxt2[...]
-        acc2 = sweep(target2, column_norms(target2), range(PREV, 8), zero)
+        target2_norms = column_norms(target2)
+        acc2 = sweep(target2, target2_norms, range(XPREV, 8), zero)
         for q in g_xprev:
             q.start()
+        acc = sweep(target, target_norms, range(PREV, XPREV), acc)
+        acc2 = sweep(target2, target2_norms, range(PREV, XPREV), acc2)
         for q in g_prev:
             q.start()
         rsum[OWN + c] += flat(mine_acc)

time: 51.3 us -> 51 us (level)
  no operation moved by 1% of the time
where the time goes in v5:
time: 51 us; the launch traced here: 50.8 us
  Pallas kernels  49.2 us (96%)
  local copies, waits for them, and re-layouts  1.61 us (3%)
    pallas_call x1, Pallas kernels, body(): pl.pallas_call(functools.partial(kernel, n_blk, block, width), out_shape=...  49.2 us
    unnamed x3, local copies, waits for them, and re-layouts  1.61 us

profile of v5, /device:TPU:1, one launch (start us, length us, event | category | flops | bytes accessed | tf_op | source)
XLA Modules:
  0.0 50.8 jit_solution(17839039336601362785)
XLA Ops:
  0.0 0.0 copy-start
  0.0 1.0 %copy-done = bf16[256,1024]{1,0:T(8,128)(2,1)S(1)} copy-done((bf16[256,1024]{1,0:T(8,128)(2,1)S(1)}, bf16[256,1024]{1,0:T(8,128)(2,1)}, u32[]{:S(2)}) %copy-start) | copy-done | bytes 524312
  1.0 49.2 %shard_map.17 = f32[1,256]{1,0:T(1,128)S(1)} custom-call(bf16[256,1024]{1,0:T(8,128)(2,1)S(1)} %copy-done), custom_call_target="tpu_custom_call" | custom-call | flops 2147483648 | bytes 524288 | tf_op jit(solution)/shard_map/pallas_call | solution.py:428
  50.2 0.6 %copy.3 = f32[256]{0:T(256)} copy(f32[256]{0:T(256)S(1)} %bitcast.1) | data formatting | bytes 2048
Async XLA Ops:
  0.0 1.0 %copy-start = (bf16[256,1024]{1,0:T(8,128)(2,1)S(1)}, bf16[256,1024]{1,0:T(8,128)(2,1)}, u32[]{:S(2)}) copy-start(bf16[256,1024]{1,0:T(8,128)(2,1)} %x.1) | copy-start | bytes 1572868
